TPU v7x, 128 devices: a whole 4x4x4 slice. The times are simulated.
128 devices in a mesh: path: 32 (over y, x, core), shard: 4 (over z).
Axes of the slice: x: 4, y: 4, z: 4, core: 2. Of those that a mesh axis runs over, the one named last changes fastest.
Arguments:
- path_table: int32 [32, 2], replicated, may hold values from 0 to 7, as said below
- master: float32 [16, 4096, 2048], P(None, 'path', 'shard'), may hold values from -0.09375 to 0.09375
- momentum: float32 [16, 4096, 2048], P(None, 'path', 'shard'), may hold values from -0.06 to 0.06
- deltas: bfloat16 [32, 2, 4096, 2048], P('path', None, None, 'shard'), may hold values from -0.059814453 to 0.059814453
- activations: bfloat16 [32768, 4096], P(('path', 'shard')), may hold values from -6 to 6
Outputs:
- new_master: float32 [16, 4096, 2048], P(None, 'path', 'shard')
- path_out: bfloat16 [32768, 4096], P(('path', 'shard'))
Inputs may be any that keep to these rules, and one draw needn't show every extreme that they name: `path_table`: at every level each of the 8 choices is named by at least one path.
All inputs are finite; a program needn't handle non-finite values.
Results may differ from a plain program's by a relative error of at most 0.014.
Values may be sent and summed in bfloat16 or wider, within the bound.
A program may use at most 192 MiB of HBM per device.

v0:
```python
import jax
import jax.numpy as jnp
from jax import lax
from jax.sharding import PartitionSpec as P


def per_device(path_table, master, momentum, deltas, activations):
    path_count = lax.axis_size("path")
    levels = deltas.shape[1]
    modules = master.shape[0]
    choices_count = modules // levels
    state_rows = master.shape[1]
    columns = master.shape[2]
    received = lax.all_to_all(deltas, "path", split_axis=2, concat_axis=0, tiled=True)
    module_of = path_table + (jnp.arange(levels, dtype=jnp.int32) * choices_count)[None, :]
    picks = jnp.arange(modules, dtype=jnp.int32)[:, None] == module_of.reshape(-1)[None, :]
    picks_half = picks.astype(jnp.bfloat16)
    sums = jnp.dot(
        picks_half,
        received.reshape(path_count * levels, state_rows * columns),
        preferred_element_type=jnp.float32,
    ).reshape(modules, state_rows, columns)
    counts = jnp.sum(picks.astype(jnp.float32), axis=1)
    grad = sums / counts[:, None, None]
    new_momentum = 0.9 * momentum + grad
    new_master = master - 0.7 * (grad + 0.9 * new_momentum)
    fresh = new_master.astype(jnp.bfloat16)
    outgoing = jnp.dot(
        picks_half.T,
        fresh.reshape(modules, state_rows * columns),
        preferred_element_type=jnp.float32,
    ).astype(jnp.bfloat16)
    outgoing = outgoing.reshape(path_count, levels, state_rows, columns)
    xf = activations.astype(jnp.float32)
    normed = (xf * lax.rsqrt(jnp.mean(xf * xf, axis=1, keepdims=True) + 1e-06)).astype(jnp.bfloat16)
    assembled = lax.all_to_all(outgoing, "path", split_axis=0, concat_axis=2, tiled=True)
    w_up = assembled[0, 0]
    hidden = jax.nn.silu(
        jnp.dot(
            lax.all_gather(normed, "shard", axis=0, tiled=True),
            w_up,
            preferred_element_type=jnp.float32,
        )
    ).astype(jnp.bfloat16)
    w_down = assembled[0, 1]
    summed = lax.psum_scatter(
        lax.dot_general(
            hidden, w_down, (((1,), (1,)), ((), ())), preferred_element_type=jnp.float32
        ).astype(jnp.bfloat16),
        "shard",
        scatter_dimension=0,
        tiled=True,
    ).astype(jnp.float32)
    return (new_master, (xf + summed).astype(jnp.bfloat16))


def solution(mesh):
    placed = (
        P(),
        P(None, "path", "shard"),
        P(None, "path", "shard"),
        P("path", None, None, "shard"),
        P(("path", "shard"), None),
    )
    return jax.shard_map(
        per_device,
        mesh=mesh,
        in_specs=placed,
        out_specs=(P(None, "path", "shard"), P(("path", "shard"), None)),
        check_vma=False,
    )
```

profile of v0, /device:TPU:1, one launch (start us, length us, event | category | flops | bytes accessed | tf_op | source)
XLA Modules:
  0.0 397.6 jit_solution(8129738976087769088)
XLA Ops:
  7.2 16.4 %copy.20 = bf16[1,2,4096,512]{3,1,0,2:T(2,128)(2,1)} copy(bf16[1,2,4096,512]{3,2,1,0:T(8,128)(2,1)} %param.8) | data formatting | bytes 16777216 | tf_op args[3]
  23.6 0.0 copy-start
  23.6 8.8 %all-to-all-start = ((bf16[1,2,4096,512]{3,1,0,2:T(2,128)(2,1)}), bf16[1,2,4096,512]{3,1,0,2:T(2,128)(2,1)}, u32[]{:S(2)}, u32[]{:S(2)}) async-start(bf16[1,2,4096,512]{3,1,0,2:T(2,128)(2,1)} %copy.20), calls=%async_computation | async-start | bytes 16777216 | tf_op jit(solution)/shard_map/all_to_all | solution.py:14
  32.4 0.0 copy-start.2
  32.4 0.0 all-gather.2.cloned.1.call-start
  32.4 0.0 copy-done
  32.5 0.5 fusion.3
  33.0 1.9 fusion.4
  34.9 0.0 all-gather.2.cloned.1.call-update
  34.9 0.0 reduce-scatter.2.cloned.1.call-start
  35.0 0.0 copy-done.2
  35.0 0.1 broadcast_add_fusion
  35.0 0.1 copy.19
  35.1 0.1 eq.16
  35.2 0.1 convert_reduce_fusion
  35.4 96.8 %all-to-all-done = bf16[1,2,4096,512]{3,1,0,2:T(2,128)(2,1)} async-done(((bf16[1,2,4096,512]{3,1,0,2:T(2,128)(2,1)}), bf16[1,2,4096,512]{3,1,0,2:T(2,128)(2,1)}, u32[]{:S(2)}, u32[]{:S(2)}) %all-to-all-start) | async-done | bytes 8388640 | tf_op jit(solution)/shard_map/all_to_all | solution.py:14
  132.1 8.7 %copy.21 = bf16[1,2,32,128,512]{4,3,1,2,0:T(8,128)(2,1)} copy(bf16[1,2,32,128,512]{4,1,3,2,0:T(2,128)(2,1)} %bitcast.1) | data formatting | bytes 16777216 | tf_op jit(solution)/shard_map/all_to_all | solution.py:14
  140.8 16.7 %copy_subtract_fusion = f32[16,128,512]{2,0,1:T(8,128)S(1)} fusion(f32[16,128,512]{2,1,0:T(8,128)} %param.6, f32[16,128,512]{2,1,0:T(8,128)} %param.7, f32[16]{0:T(128)S(1)} %convert_reduce_fusion, s32[64]{0:T(128)S(1)} %eq.16, bf16[8,8,128,512]{3,2,1,0:T(8,128)(2,1)} %bitcast.46), kind=kOutput, calls=%fused_computation.14 | convolution fusion | flops 141558784 | bytes 20971840 | tf_op jit(solution)/shard_map/dot_general | solution.py:18
  157.5 0.0 copy-start.1
  157.5 0.3 convert_bitcast_fusion
  157.9 0.2 copy.29
  158.0 1.5 copy-done.1
  159.6 5.6 %convolution_convert_fusion = bf16[64,65536]{1,0:T(8,128)(2,1)} fusion(bf16[16,65536]{1,0:T(8,128)(2,1)S(1)} %bitcast.47, s32[64]{0:T(128)S(1)} %eq.16), kind=kOutput, calls=%fused_computation | convolution fusion | flops 138413056 | bytes 10486016 | tf_op jit(solution)/shard_map/dot_general | solution.py:28
  165.2 9.9 %copy.31 = bf16[8,8,128,512]{3,2,1,0:T(8,128)(2,1)} copy(bf16[8,8,128,512]{3,1,2,0:T(8,128)(2,1)} %bitcast.43) | data formatting | bytes 16777216
  175.0 107.0 %all_to_all.33 = bf16[32,2,128,512]{3,2,1,0:T(8,128)(2,1)} all-to-all(bf16[32,2,128,512]{3,2,1,0:T(8,128)(2,1)} %bitcast.44), channel_id=1, replica_groups=mesh['path'=32,'shard'=4] {'path'}, dimensions={0} | all-to-all | bytes 16777216 | tf_op jit(solution)/shard_map/all_to_all | solution.py:36
  282.0 7.6 %copy.26 = bf16[32,2,128,512]{3,2,0,1:T(8,128)(2,1)} copy(bf16[32,2,128,512]{3,2,1,0:T(8,128)(2,1)} %all_to_all.33) | data formatting | bytes 16777216 | tf_op jit(solution)/shard_map/all_to_all | solution.py:36
  289.6 0.0 all-gather.2.cloned.1.call-done
  289.6 15.9 %convolution_convert_fusion.1 = bf16[1024,4096]{1,0:T(8,128)(2,1)} fusion(bf16[1,2,4096,512]{3,2,1,0:T(8,128)(2,1)} %bitcast.45, bf16[1024,4096]{1,0:T(8,128)(2,1)} %all-gather.2.cloned.1.call-done), kind=kOutput, calls=%fused_computation.4 | convolution fusion | flops 8596750336 | bytes 25165824 | tf_op jit(solution)/shard_map/dot_general | solution.py:47
  305.6 0.0 reduce-scatter.2.cloned.1.call-update
  305.6 6.6 %copy.27 = f32[16,128,512]{2,1,0:T(8,128)} copy(f32[16,128,512]{2,0,1:T(8,128)} %copy-done.1) | data formatting | bytes 8388608
  312.2 74.8 %reduce-scatter.2.cloned.1.call-done = bf16[256,4096]{1,0:T(8,128)(2,1)} async-done(((bf16[1024,4096]{1,0:T(8,128)(2,1)}), bf16[256,4096]{1,0:T(8,128)(2,1)}) %reduce-scatter.2.cloned.1.call-update) | async-done | bytes 2097168 | tf_op jit(solution)/shard_map/reduce_scatter | solution.py:46
  387.1 3.7 fusion.5
  (2 shorter events, 0.0 us)
Async XLA Ops:
  23.6 8.9 %copy-start = (bf16[256,4096]{1,0:T(8,128)(2,1)S(1)}, bf16[256,4096]{1,0:T(8,128)(2,1)}, u32[]{:S(2)}) copy-start(bf16[256,4096]{1,0:T(8,128)(2,1)} %param.9) | copy-start | bytes 6291460
  23.6 108.5 %all-to-all-start = ((bf16[1,2,4096,512]{3,1,0,2:T(2,128)(2,1)}), bf16[1,2,4096,512]{3,1,0,2:T(2,128)(2,1)}, u32[]{:S(2)}, u32[]{:S(2)}) async-start(bf16[1,2,4096,512]{3,1,0,2:T(2,128)(2,1)} %copy.20), calls=%async_computation | async-start | bytes 16777216 | tf_op jit(solution)/shard_map/all_to_all | solution.py:14
  32.4 2.6 copy-start.2
  32.4 257.2 %all-gather.2.cloned.1.call-start = ((), (), s32[]{:S(2)}) async-start(), calls=%async_computation.3 | async-start | bytes 10485760 | tf_op jit(solution)/shard_map/all_gather | solution.py:40
  34.9 352.2 %reduce-scatter.2.cloned.1.call-start = ((), (), s32[]{:S(2)}) async-start(), calls=%async_computation.4 | async-start | bytes 10485760 | tf_op jit(solution)/shard_map/reduce_scatter | solution.py:46
  157.5 2.0 copy-start.1
Sparse Core Ops, SparseCore 0:
  35.5 85.3 all-gather.1
  305.7 81.2 reduce-scatter.1
where the time goes:
time: 398 us
  waiting for transfers between devices  172 us (43%)
  blocking collectives  107 us (27%)
  local copies, waits for them, and re-layouts  51.1 us (13%)
  matrix products  38.2 us (10%)
  between operations  14.1 us (4%)
  starting transfers between devices  8.87 us (2%)
  other arithmetic  6.63 us (2%)
    all_to_all x1, blocking collectives, per_device(): lax.all_to_all(outgoing, 'path', split_axis=0, concat_axis=2, tiled=True)  107 us
    all_to_all x1, waiting for transfers between devices, per_device(): lax.all_to_all(deltas, 'path', split_axis=2, concat_axis=0, tiled=True)  96.8 us
    reduce_scatter x1, waiting for transfers between devices, per_device(): lax.psum_scatter(lax.dot_general(hidden, w_down, (((1,), (1,)), ((), ()))...  74.8 us
    unnamed x9, local copies, waits for them, and re-layouts  34.5 us
    dot_general x1, matrix products, per_device(): jnp.dot(picks_half, received.reshape(path_count * levels, state_rows * co...  16.7 us
    dot_general x1, matrix products, per_device(): lax.dot_general(hidden, w_down, (((1,), (1,)), ((), ())), preferred_eleme...  15.9 us
    all_to_all x1, starting transfers between devices, per_device(): lax.all_to_all(deltas, 'path', split_axis=2, concat_axis=0, tiled=True)  8.78 us
    all_to_all x1, local copies, waits for them, and re-layouts, per_device(): lax.all_to_all(deltas, 'path', split_axis=2, concat_axis=0, tiled=True)  8.69 us
  transfers between devices with their start and end apart: 3, of which 2 were waited for; matrix products, arithmetic and copies ran while one was open for 15% of the time, Pallas kernels for 0%

commit v1 on v0

v1 whole, which is shorter than its diff:
```python
import functools

import jax
import jax.numpy as jnp
from jax import lax
from jax.experimental import pallas as pl
from jax.experimental.pallas import tpu as pltpu
from jax.sharding import PartitionSpec as P

MESH = pl.DeviceIdType.MESH
F32 = jnp.float32
BF16 = jnp.bfloat16

TILE = 16
BIG = 32


def kernel(
    mods, wts, master, momentum, deltas, acts,
    nm_out, out,
    nrm, xbuf, xacc, mast, mom, rec0, rec1, fresh, wup, wdn, hid, parts,
    far_l, far_r, from_l, from_r,
    sem_a0, sem_a1, sem_b0, sem_b1,
    snd_a0, snd_a1, snd_b0, snd_b1,
    ag_snd, ag_l, ag_r, ag_f,
    rs_snd, rs_fl, rs_fr, rs_l, rs_r,
    sem_in, sem_out,
):
    n_path = rec0.shape[0]
    n_shard = nrm.shape[0]
    rows = rec0.shape[1]
    cols = rec0.shape[2]
    choices = fresh.shape[0]
    chunks0 = rows // BIG
    chunks1 = rows // TILE
    tokens = nrm.shape[1]
    half = tokens // 2
    me = lax.axis_index("path")
    z = lax.axis_index("shard")
    right = lax.rem(z + 1, n_shard)
    left = lax.rem(z + n_shard - 1, n_shard)

    def peer(i):
        j = lax.rem(i * 11, n_path)
        core = lax.rem(me + j, 2)
        x = lax.rem(me // 2 + j // 2, 4)
        y = lax.rem(me // 8 + j // 8, n_path // 8)
        return (y * 4 + x) * 2 + core

    load_x = pltpu.make_async_copy(acts, xbuf, sem_in.at[0])
    load_x.start()
    load_m = pltpu.make_async_copy(master, mast, sem_in.at[1])
    load_m.start()
    load_v = pltpu.make_async_copy(momentum, mom, sem_in.at[2])
    load_v.start()

    barrier = pltpu.get_barrier_semaphore()

    @pl.loop(1, n_path)
    def _(i):
        pl.semaphore_signal(barrier, inc=1, device_id={"path": peer(i)}, device_id_type=MESH)

    for side in (left, right):
        pl.semaphore_signal(barrier, inc=1, device_id={"shard": side}, device_id_type=MESH)
    pl.semaphore_wait(barrier, n_path - 1 + 2)

    def slice1(owner, c):
        return lax.rem(owner + c, chunks1)

    def send_a0(c):
        def src(q):
            return deltas.at[0, 0, pl.ds(pl.multiple_of(q * rows + c * BIG, BIG), BIG)]

        dst = rec0.at[me, pl.ds(c * BIG, BIG)]

        @pl.loop(1, n_path)
        def _(i):
            q = peer(i)
            pltpu.make_async_remote_copy(
                src(q), dst, snd_a0.at[c], sem_a0.at[c], device_id={"path": q}, device_id_type=MESH
            ).start()

        pltpu.make_async_copy(src(me), dst, sem_a0.at[c]).start()

    def send_a1(c):
        def src(q):
            return deltas.at[0, 1, pl.ds(pl.multiple_of(q * rows + slice1(q, c) * TILE, TILE), TILE)]

        dst = rec1.at[c, me]

        @pl.loop(1, n_path)
        def _(i):
            q = peer(i)
            pltpu.make_async_remote_copy(
                src(q), dst, snd_a1.at[c], sem_a1.at[c], device_id={"path": q}, device_id_type=MESH
            ).start()

        pltpu.make_async_copy(src(me), dst, sem_a1.at[c]).start()

    def send_b0(c):
        span = pl.ds(c * BIG, BIG)
        dst = wup.at[me, span]

        @pl.loop(1, n_path)
        def _(i):
            q = peer(i)
            pltpu.make_async_remote_copy(
                rec0.at[q, span], dst, snd_b0.at[c], sem_b0.at[c], device_id={"path": q}, device_id_type=MESH
            ).start()

        pltpu.make_async_copy(rec0.at[me, span], dst, sem_b0.at[c]).start()

    def send_b1(c):
        dst = wdn.at[c, (me // chunks1) * chunks1 + slice1(me, c)]

        @pl.loop(1, n_path)
        def _(i):
            q = peer(i)
            pltpu.make_async_remote_copy(
                rec1.at[c, q], dst, snd_b1.at[c], sem_b1.at[c], device_id={"path": q}, device_id_type=MESH
            ).start()

        pltpu.make_async_copy(rec1.at[c, me], dst, sem_b1.at[c]).start()

    def wait_like(ref, sem):
        pltpu.make_async_copy(ref, ref, sem).wait()

    def combine(level, take, put, state_row):
        at = pl.ds(state_row, TILE)
        width = 256
        for part in range(cols // width):
            lanes = pl.ds(part * width, width)

            def add(p, sums):
                value = take(p, lanes).astype(F32)
                return tuple(
                    total + wts[(level * n_path + p) * choices + m] * value for m, total in enumerate(sums)
                )

            grads = lax.fori_loop(
                0, n_path, add, tuple(jnp.zeros((TILE, width), F32) for _ in range(choices)), unroll=4
            )
            for m, grad in enumerate(grads):
                module = level * choices + m
                new_mom = 0.9 * mom[module, at, lanes] + grad
                new = mast[module, at, lanes] - 0.7 * (grad + 0.9 * new_mom)
                mast[module, at, lanes] = new
                fresh[m, :, lanes] = new.astype(BF16)

        @pl.loop(0, n_path, unroll=4)
        def _(p):
            put(p, fresh[mods[level * n_path + p]])

    def combine0(c):
        @pl.loop(0, BIG // TILE)
        def _(t):
            row = pl.multiple_of(c * BIG + t * TILE, TILE)

            def take(p, lanes):
                return rec0[p, pl.ds(row, TILE), lanes]

            def put(p, value):
                rec0[p, pl.ds(row, TILE), :] = value

            combine(0, take, put, row)

    def combine1(c):
        def take(p, lanes):
            return rec1[c, p, :, lanes]

        def put(p, value):
            rec1[c, p, :, :] = value

        combine(1, take, put, pl.multiple_of(slice1(me, c) * TILE, TILE))

    def z_copy(src, dst, send, recv, side):
        pltpu.make_async_remote_copy(
            src, dst, send, recv, device_id={"shard": side}, device_id_type=MESH
        ).start()

    for c in range(chunks0):
        send_a0(c)
    send_a1(0)
    send_a1(1)

    load_x.wait()

    @pl.loop(0, tokens // TILE)
    def _(t):
        at = pl.ds(pl.multiple_of(t * TILE, TILE), TILE)
        xf = xbuf[at, :].astype(F32)
        xacc[at, :] = xf
        scale = lax.rsqrt(jnp.mean(xf * xf, axis=1, keepdims=True) + 1e-06)
        nrm[z, at, :] = (xf * scale).astype(BF16)

    top, low = pl.ds(0, half), pl.ds(half, half)
    z_copy(nrm.at[z, top], nrm.at[z, top], ag_snd.at[0], ag_l.at[0], right)
    z_copy(nrm.at[z, low], nrm.at[z, low], ag_snd.at[1], ag_r.at[1], left)
    z_copy(nrm.at[z, low], nrm.at[z, low], ag_snd.at[2], ag_l.at[1], right)
    z_copy(nrm.at[z, top], nrm.at[z, top], ag_snd.at[3], ag_r.at[0], left)
    far = lax.rem(z + 2, n_shard)

    load_m.wait()
    load_v.wait()
    for c in range(chunks0):
        wait_like(rec0.at[:, pl.ds(c * BIG, BIG)], sem_a0.at[c])
        combine0(c)
        send_b0(c)
        if c == chunks0 - 2:
            wait_like(nrm.at[left, top], ag_l.at[0])
            z_copy(nrm.at[left, top], nrm.at[left, top], ag_snd.at[4], ag_f.at[0], right)
            wait_like(nrm.at[right, low], ag_r.at[1])
            z_copy(nrm.at[right, low], nrm.at[right, low], ag_snd.at[5], ag_f.at[1], left)
    state0 = pltpu.make_async_copy(mast.at[pl.ds(0, choices)], nm_out.at[pl.ds(0, choices)], sem_out.at[0])
    state0.start()

    def step_a1(c):
        wait_like(rec1.at[c], sem_a1.at[c])
        combine1(c)
        send_b1(c)
        if c + 2 < chunks1:
            send_a1(c + 2)

    def rs_first(c):
        wait_like(wdn.at[c], sem_b1.at[c])
        value = lax.dot_general(
            hid[...].reshape(n_shard * tokens, cols),
            wdn[c].reshape(n_path * TILE, cols),
            (((1,), (1,)), ((), ())),
            preferred_element_type=F32,
        ).astype(BF16)
        parts[c] = value.reshape(n_shard, tokens, n_path * TILE)
        z_copy(parts.at[c, 2, top], far_l.at[c], rs_snd.at[c], rs_fl.at[c], right)
        z_copy(parts.at[c, 2, low], far_r.at[c], rs_snd.at[c], rs_fr.at[c], left)
        z_copy(parts.at[c, 1, low], from_l.at[c, low], rs_snd.at[c], rs_l.at[c], right)
        z_copy(parts.at[c, 3, top], from_r.at[c, top], rs_snd.at[c], rs_r.at[c], left)

    def rs_second(c):
        wait_like(far_l.at[c], rs_fl.at[c])
        parts[c, 1, 0:half, :] = (parts[c, 1, 0:half, :].astype(F32) + far_l[c].astype(F32)).astype(BF16)
        z_copy(parts.at[c, 1, top], from_l.at[c, top], rs_snd.at[c], rs_l.at[c], right)
        wait_like(far_r.at[c], rs_fr.at[c])
        parts[c, 3, half:tokens, :] = (parts[c, 3, half:tokens, :].astype(F32) + far_r[c].astype(F32)).astype(BF16)
        z_copy(parts.at[c, 3, low], from_r.at[c, low], rs_snd.at[c], rs_r.at[c], left)

    def rs_last(c):
        wait_like(from_l.at[c], rs_l.at[c])
        wait_like(from_r.at[c], rs_r.at[c])
        group = lax.broadcasted_iota(jnp.int32, (TILE, 128), 1) // TILE

        @pl.loop(0, tokens // TILE)
        def _(t):
            at = pl.ds(pl.multiple_of(t * TILE, TILE), TILE)
            for g in range(n_path // chunks1):
                lanes = pl.ds(g * 128, 128)
                total = (
                    parts[c, 0, at, lanes].astype(F32)
                    + from_l[c, at, lanes].astype(F32)
                    + from_r[c, at, lanes].astype(F32)
                )
                for q in range(chunks1):
                    lane = pl.ds((g * chunks1 + q) * 128, 128)
                    value = xacc[at, lane] + jnp.where(group == (c + q) % chunks1, total, 0.0)
                    if c == chunks1 - 1:
                        out[at, lane] = value.astype(BF16)
                    else:
                        xacc[at, lane] = value

    step_a1(0)
    step_a1(1)

    wait_like(nrm.at[left, low], ag_l.at[1])
    wait_like(nrm.at[right, top], ag_r.at[0])
    wait_like(nrm.at[far, top], ag_f.at[0])
    wait_like(nrm.at[far, low], ag_f.at[1])
    for c in range(chunks0):
        wait_like(wup.at[:, pl.ds(c * BIG, BIG)], sem_b0.at[c])

    @pl.loop(0, n_shard)
    def _(d):
        value = jnp.dot(
            nrm[lax.rem(z + d, n_shard)], wup[...].reshape(n_path * rows, cols), preferred_element_type=F32
        )
        hid[d] = (value / (1.0 + jnp.exp(-value))).astype(BF16)

    for c in range(chunks1):
        rs_first(c)
        if c >= 1:
            rs_second(c - 1)
        if c >= 2:
            rs_last(c - 2)
        if c + 2 < chunks1:
            step_a1(c + 2)
        if c + 2 == chunks1 - 1:
            state1 = pltpu.make_async_copy(
                mast.at[pl.ds(choices, choices)], nm_out.at[pl.ds(choices, choices)], sem_out.at[1]
            )
            state1.start()
    rs_second(chunks1 - 1)
    rs_last(chunks1 - 2)
    rs_last(chunks1 - 1)

    others = pl.ds(0, n_path - 1)
    for c in range(chunks0):
        wait_like(rec0.at[others, pl.ds(c * BIG, BIG)], snd_a0.at[c])
        wait_like(rec0.at[others, pl.ds(c * BIG, BIG)], snd_b0.at[c])
    for c in range(chunks1):
        wait_like(rec1.at[c, others], snd_a1.at[c])
        wait_like(rec1.at[c, others], snd_b1.at[c])
        wait_like(parts.at[c, pl.ds(0, 3)], rs_snd.at[c])
    for k in range(6):
        wait_like(nrm.at[0, top], ag_snd.at[k])
    state0.wait()
    state1.wait()


def per_device(path_table, master, momentum, deltas, activations):
    n_path = lax.axis_size("path")
    n_shard = lax.axis_size("shard")
    levels = deltas.shape[1]
    modules, rows, cols = master.shape
    choices = modules // levels
    tokens, width = activations.shape
    chunks0, chunks1 = rows // BIG, rows // TILE
    table = path_table.T
    picks = (table[:, :, None] == jnp.arange(choices, dtype=jnp.int32)[None, None, :]).astype(F32)
    wts = picks / jnp.sum(picks, axis=1, keepdims=True)
    hbm = pl.BlockSpec(memory_space=pl.ANY)
    smem = pl.BlockSpec(memory_space=pltpu.SMEM)
    dma = pltpu.SemaphoreType.DMA
    block = n_path * TILE
    return tuple(pl.pallas_call(
        kernel,
        out_shape=(
            jax.ShapeDtypeStruct((modules, rows, cols), F32),
            jax.ShapeDtypeStruct((tokens, width), BF16),
        ),
        in_specs=[smem, smem, hbm, hbm, hbm, hbm],
        out_specs=(hbm, pl.BlockSpec(memory_space=pltpu.VMEM)),
        scratch_shapes=[
            pltpu.VMEM((n_shard, tokens, width), BF16),
            pltpu.VMEM((tokens, width), BF16),
            pltpu.VMEM((tokens, width), F32),
            pltpu.VMEM((modules, rows, cols), F32),
            pltpu.VMEM((modules, rows, cols), F32),
            pltpu.VMEM((n_path, rows, cols), BF16),
            pltpu.VMEM((chunks1, n_path, TILE, cols), BF16),
            pltpu.VMEM((choices, TILE, cols), BF16),
            pltpu.VMEM((n_path, rows, cols), BF16),
            pltpu.VMEM((chunks1, n_path, TILE, cols), BF16),
            pltpu.VMEM((n_shard, tokens, cols), BF16),
            pltpu.VMEM((chunks1, n_shard, tokens, block), BF16),
            pltpu.VMEM((chunks1, tokens // 2, block), BF16),
            pltpu.VMEM((chunks1, tokens // 2, block), BF16),
            pltpu.VMEM((chunks1, tokens, block), BF16),
            pltpu.VMEM((chunks1, tokens, block), BF16),
            dma((chunks0,)), dma((chunks1,)), dma((chunks0,)), dma((chunks1,)),
            dma((chunks0,)), dma((chunks1,)), dma((chunks0,)), dma((chunks1,)),
            dma((6,)), dma((2,)), dma((2,)), dma((2,)),
            dma((chunks1,)), dma((chunks1,)), dma((chunks1,)), dma((chunks1,)), dma((chunks1,)),
            dma((3,)), dma((2,)),
        ],
        compiler_params=pltpu.CompilerParams(
            collective_id=0, has_side_effects=True, vmem_limit_bytes=62 * 1024 * 1024
        ),
    )(table.reshape(-1), wts.reshape(-1), master, momentum, deltas, activations))


def solution(mesh):
    placed = (
        P(),
        P(None, "path", "shard"),
        P(None, "path", "shard"),
        P("path", None, None, "shard"),
        P(("path", "shard"), None),
    )
    return jax.shard_map(
        per_device,
        mesh=mesh,
        in_specs=placed,
        out_specs=(P(None, "path", "shard"), P(("path", "shard"), None)),
        check_vma=False,
    )
```

time: 398 us -> 224 us (0.56)
  Pallas kernels: 0 us -> 214 us
  waiting for transfers between devices: 172 us -> 0 us
  blocking collectives: 107 us -> 0 us
  local copies, waits for them, and re-layouts: 51.1 us -> 8.22 us
  matrix products: 38.2 us -> 0 us
  between operations: 14.1 us -> 0.65 us
  starting transfers between devices: 8.87 us -> 0 us
  other arithmetic: 6.63 us -> 0.88 us
    pallas_call x0 -> x1, Pallas kernels: none -> 214 us  [per_device(): pl.pallas_call(kernel, out_shape=(jax.ShapeDtypeStruct((modules, rows, co...]
    all_to_all x1 -> x0, blocking collectives: 107 us -> none  [per_device(): lax.all_to_all(outgoing, 'path', split_axis=0, concat_axis=2, tiled=True)]
    all_to_all x1 -> x0, waiting for transfers between devices: 96.8 us -> none  [per_device(): lax.all_to_all(deltas, 'path', split_axis=2, concat_axis=0, tiled=True)]
    reduce_scatter x1 -> x0, waiting for transfers between devices: 74.8 us -> none  [per_device(): lax.psum_scatter(lax.dot_general(hidden, w_down, (((1,), (1,)), ((), ()))...]
    dot_general x3 -> x0, matrix products: 38.2 us -> none  [the longest x1 16.7 us: per_device(): jnp.dot(picks_half, received.reshape(path_count * levels, state_rows * co...]
    unnamed x9 -> x4, local copies, waits for them, and re-layouts: 34.5 us -> 6.28 us
    all_to_all x2 -> x0, local copies, waits for them, and re-layouts: 16.3 us -> none  [the longest x1 8.69 us: per_device(): lax.all_to_all(deltas, 'path', split_axis=2, concat_axis=0, tiled=True)]
    all_to_all x1 -> x0, starting transfers between devices: 8.78 us -> none  [per_device(): lax.all_to_all(deltas, 'path', split_axis=2, concat_axis=0, tiled=True)]
  transfers between devices with their start and end apart: 3 -> 0, of which waited for: 2 -> 0; matrix products, arithmetic and copies ran while one was open for 15% -> 0% of each run, Pallas kernels for 0% -> 0%
where the time goes in v1:
time: 224 us; the launch traced here: 223 us
  Pallas kernels  214 us (96%)
  local copies, waits for them, and re-layouts  8.22 us (4%)
    pallas_call x1, Pallas kernels, per_device(): pl.pallas_call(kernel, out_shape=(jax.ShapeDtypeStruct((modules, rows, co...  214 us
    unnamed x4, local copies, waits for them, and re-layouts  6.28 us

profile of v1, /device:TPU:1, one launch (start us, length us, event | category | flops | bytes accessed | tf_op | source)
XLA Modules:
  0.0 223.4 jit_solution(982619314183549449)
XLA Ops:
  0.6 1.3 reshape.16.mods
  1.9 0.9 fusion.1
  2.8 0.7 div.14.wts
  3.5 213.7 %shard_map.68 = (f32[16,128,512]{2,1,0:T(8,128)}, bf16[256,4096]{1,0:T(8,128)(2,1)}) custom-call(s32[64]{0:T(128)} %reshape.16.mods, f32[512]{0:T(512)} %div.14.wts, f32[16,128,512]{2,1,0:T(8,128)} %master.1, f32[16,128,512]{2,1,0:T(8,128)} %momentum.1, bf16[1,2,4096,512]{3,2,1,0:T(8,128)(2,1)} %deltas.1, bf16[256,4096]{1,0:T(8,128)(2,1)} %acts.1), custom_call_target="tpu_custom_call" | custom-call | tf_op jit(solution)/shard_map/pallas_call | solution.py:332
  217.1 0.0 copy-start
  217.2 5.0 %copy.9 = f32[16,128,512]{2,1,0:T(8,128)} copy(f32[16,128,512]{2,1,0:T(8,128)} %get-tuple-element.4) | data formatting | bytes 8388608
  222.1 0.0 copy-done
  222.1 1.3 copy.10
Async XLA Ops:
  217.1 5.0 %copy-start = (bf16[256,4096]{1,0:T(8,128)(2,1)S(1)}, bf16[256,4096]{1,0:T(8,128)(2,1)}, u32[]{:S(2)}) copy-start(bf16[256,4096]{1,0:T(8,128)(2,1)} %get-tuple-element.5) | copy-start | bytes 6291460

commit v2 on v0

v2 whole, which is shorter than its diff:
```python
import jax
import jax.numpy as jnp
from jax import lax
from jax.experimental import pallas as pl
from jax.experimental.pallas import tpu as pltpu
from jax.sharding import PartitionSpec as P

MESH = pl.DeviceIdType.MESH
F32 = jnp.float32
BF16 = jnp.bfloat16

TILE = 16
SLOTS = 4
AHEAD = 3
SIDE = 4


def kernel(
    table, master, momentum, deltas, acts,
    state, out,
    wts, counts,
    nrm, momb, rec, part, far, frm, dense, pick, wup, wdn, hid, rs_far, rs_frm,
    s_a, s_far, s_frm, s_bi, s_bf, s_b,
    o_a, o_p, o_bi, o_b,
    ag_snd, ag_l, ag_r, ag_f,
    rs_snd, s_rfar, s_rfrm,
    sem_in, sem_mom,
):
    levels = deltas.shape[0]
    rows = deltas.shape[4]
    cols = deltas.shape[5]
    jobs = rec.shape[0]
    per_level = jobs // levels
    choices = dense.shape[3]
    group = rec.shape[2]
    n_path = SIDE * group
    n_shard, tokens, width = nrm.shape
    half = tokens // 2
    some = choices // 2
    lanes_of = [pl.ds(t * (cols // 2), cols // 2) for t in range(2)]
    block = n_path * TILE

    me = lax.axis_index("path")
    z = lax.axis_index("shard")
    core = lax.rem(me, 2)
    x = lax.rem(me // 2, SIDE)
    y = me // group
    right = lax.rem(z + 1, n_shard)
    left = lax.rem(z + n_shard - 1, n_shard)
    direct = (y, x)
    ring = (x, y)

    def path_of(t, d, r, c):
        return (d * SIDE + r) * 2 + c if t == 0 else (r * SIDE + d) * 2 + c

    def member(t, s):
        return path_of(t, s // 2, ring[t], s % 2)

    def offset(i):
        return lax.rem(i * 3, group)

    def direct_slot(t, i):
        j = offset(i)
        return lax.rem(direct[t] + j // 2, SIDE) * 2 + lax.rem(core + j, 2)

    def direct_peer(t, slot):
        return path_of(t, slot // 2, ring[t], lax.rem(slot, 2))

    ring_up = [path_of(t, direct[t], lax.rem(ring[t] + 1, SIDE), core) for t in range(2)]
    ring_down = [path_of(t, direct[t], lax.rem(ring[t] + SIDE - 1, SIDE), core) for t in range(2)]

    load_x = pltpu.make_async_copy(acts, out, sem_in.at[0])
    load_x.start()
    load_m = pltpu.make_async_copy(master, state, sem_in.at[1])
    load_m.start()

    barrier = pltpu.get_barrier_semaphore()

    @pl.loop(1, group)
    def _(i):
        slot = direct_slot(0, i)
        pl.semaphore_signal(barrier, inc=1, device_id={"path": direct_peer(0, slot)}, device_id_type=MESH)

    @pl.loop(2, group)
    def _(i):
        slot = lax.rem(direct[1] + i // 2, SIDE) * 2 + lax.rem(core + i, 2)
        pl.semaphore_signal(barrier, inc=1, device_id={"path": direct_peer(1, slot)}, device_id_type=MESH)

    for side in (left, right):
        pl.semaphore_signal(barrier, inc=1, device_id={"shard": side}, device_id_type=MESH)
    pl.semaphore_wait(barrier, (group - 1) + (group - 2) + 2)

    def wait_like(ref, sem):
        pltpu.make_async_copy(ref, ref, sem).wait()

    def p_copy(src, dst, send, recv, peer):
        pltpu.make_async_remote_copy(
            src, dst, send, recv, device_id={"path": peer}, device_id_type=MESH
        ).start()

    def z_copy(src, dst, send, recv, side):
        pltpu.make_async_remote_copy(
            src, dst, send, recv, device_id={"shard": side}, device_id_type=MESH
        ).start()

    def rows_of(j):
        return pl.ds(pl.multiple_of(lax.rem(j, per_level) * TILE, TILE), TILE)

    def send_deltas(j):
        level = j // per_level
        at = rows_of(j)

        def src(t, slot):
            d, c = slot // 2, lax.rem(slot, 2)
            if t == 0:
                return deltas.at[level, d, :, c, at, lanes_of[0]]
            return deltas.at[level, :, d, c, at, lanes_of[1]]

        def dst(t):
            return rec.at[j, t, direct[t] * 2 + core]

        @pl.loop(1, group)
        def _(i):
            for t in range(2):
                slot = direct_slot(t, i)
                p_copy(src(t, slot), dst(t), o_a.at[0], s_a.at[j, t], direct_peer(t, slot))

        for t in range(2):
            pltpu.make_async_copy(src(t, direct[t] * 2 + core), dst(t), s_a.at[j, t]).start()

    def sums(j, t, owner):
        base = (j // per_level) * n_path
        total = [None] * choices
        for s in range(group):
            value = rec[j, t, s, owner].astype(F32)
            at = (base + member(t, s)) * choices
            for m in range(choices):
                term = wts[at + m] * value
                total[m] = term if total[m] is None else total[m] + term
        return total

    def momentum_copy(j):
        level = j // per_level
        slot = lax.rem(j, SLOTS)
        return pltpu.make_async_copy(
            momentum.at[pl.ds(level * choices, choices), rows_of(j)], momb.at[slot], sem_mom.at[slot]
        )

    first, second = pl.ds(0, some), pl.ds(some, some)

    def step1(j):
        slot = lax.rem(j, SLOTS)

        @pl.when(j >= SLOTS)
        def _():
            wait_like(part.at[slot], o_p.at[j - SLOTS])

        momentum_copy(j).start()
        for t in range(2):
            wait_like(rec.at[j, t], s_a.at[j, t])

        def fill(t, k):
            for m, value in enumerate(sums(j, t, lax.rem(ring[t] + k, SIDE))):
                part[slot, t, k - 1, m] = value.astype(BF16)

        for t in range(2):
            fill(t, 2)
            p_copy(part.at[slot, t, 1, first], far.at[j, t, 0], o_p.at[j], s_far.at[j, t, 0], ring_up[t])
            p_copy(part.at[slot, t, 1, second], far.at[j, t, 1], o_p.at[j], s_far.at[j, t, 1], ring_down[t])
        for t in range(2):
            fill(t, 1)
            p_copy(part.at[slot, t, 0, second], frm.at[j, t, 0, second], o_p.at[j], s_frm.at[j, t, 0], ring_up[t])
            fill(t, 3)
            p_copy(part.at[slot, t, 2, first], frm.at[j, t, 1, first], o_p.at[j], s_frm.at[j, t, 1], ring_down[t])

    def step2(j):
        slot = lax.rem(j, SLOTS)
        for t in range(2):
            wait_like(far.at[j, t, 0], s_far.at[j, t, 0])
            for m in range(some):
                part[slot, t, 0, m] = (part[slot, t, 0, m].astype(F32) + far[j, t, 0, m].astype(F32)).astype(BF16)
            p_copy(part.at[slot, t, 0, first], frm.at[j, t, 0, first], o_p.at[j], s_frm.at[j, t, 0], ring_up[t])
            wait_like(far.at[j, t, 1], s_far.at[j, t, 1])
            for m in range(some):
                n = some + m
                part[slot, t, 2, n] = (part[slot, t, 2, n].astype(F32) + far[j, t, 1, m].astype(F32)).astype(BF16)
            p_copy(part.at[slot, t, 2, second], frm.at[j, t, 1, second], o_p.at[j], s_frm.at[j, t, 1], ring_down[t])

    def step3(j):
        level = j // per_level
        slot = lax.rem(j, SLOTS)
        at = rows_of(j)
        momentum_copy(j).wait()
        for t in range(2):
            wait_like(frm.at[j, t, 0], s_frm.at[j, t, 0])
            wait_like(frm.at[j, t, 1], s_frm.at[j, t, 1])
            for m, total in enumerate(sums(j, t, ring[t])):
                module = level * choices + m
                total = total + frm[j, t, 0, m].astype(F32) + frm[j, t, 1, m].astype(F32)
                grad = total / jnp.full(total.shape, counts[module], F32)
                new_mom = 0.9 * momb[slot, m, :, lanes_of[t]] + grad
                new = state[module, at, lanes_of[t]] - 0.7 * (grad + 0.9 * new_mom)
                state[module, at, lanes_of[t]] = new
                dense[j, t, 0, m] = new.astype(BF16)
            own = dense.at[j, t, 0]
            p_copy(own.at[first], dense.at[j, t, 3, first], o_bi.at[0], s_bf.at[j, t, 0], ring_up[t])
            p_copy(own.at[second], dense.at[j, t, 1, second], o_bi.at[0], s_bf.at[j, t, 1], ring_down[t])
            p_copy(own.at[second], dense.at[j, t, 3, second], o_bi.at[0], s_bi.at[j, t], ring_up[t])
            p_copy(own.at[first], dense.at[j, t, 1, first], o_bi.at[0], s_bi.at[j, t], ring_down[t])

    def step4(j):
        for t in range(2):
            wait_like(dense.at[j, t, 3, first], s_bf.at[j, t, 0])
            p_copy(dense.at[j, t, 3, first], dense.at[j, t, 2, first], o_bi.at[0], s_bi.at[j, t], ring_up[t])
            wait_like(dense.at[j, t, 1, second], s_bf.at[j, t, 1])
            p_copy(dense.at[j, t, 1, second], dense.at[j, t, 2, second], o_bi.at[0], s_bi.at[j, t], ring_down[t])

    def step5(j):
        level = j // per_level
        at = rows_of(j)
        chunk = lax.rem(j, per_level)
        for t in range(2):
            wait_like(dense.at[j, t, pl.ds(0, 2)], s_bi.at[j, t])
            for k in range(SIDE):
                pick[t, k] = dense[j, t, k]

            @pl.loop(0, group)
            def _(s):
                need = table[level, direct_peer(t, s)]
                for k in range(SIDE):
                    rec[j, t, s, lax.rem(ring[t] + k, SIDE)] = pick[t, k, need]

        def send(dst):
            @pl.loop(1, group)
            def _(i):
                for t in range(2):
                    slot = direct_slot(t, i)
                    p_copy(rec.at[j, t, slot], dst(t), o_b.at[0], s_b.at[j, t], direct_peer(t, slot))

            for t in range(2):
                pltpu.make_async_copy(rec.at[j, t, direct[t] * 2 + core], dst(t), s_b.at[j, t]).start()

        @pl.when(level == 0)
        def _():
            def dst(t):
                if t == 0:
                    return wup.at[y, :, core, at, lanes_of[0]]
                return wup.at[:, x, core, at, lanes_of[1]]

            send(dst)

        @pl.when(level == 1)
        def _():
            def dst(t):
                if t == 0:
                    return wdn.at[chunk, y, :, core, :, lanes_of[0]]
                return wdn.at[chunk, :, x, core, :, lanes_of[1]]

            send(dst)

    top, low = pl.ds(0, half), pl.ds(half, half)
    opposite = lax.rem(z + 2, n_shard)

    def first_projection():
        wait_like(nrm.at[left, low], ag_l.at[1])
        wait_like(nrm.at[right, top], ag_r.at[0])
        wait_like(nrm.at[opposite, top], ag_f.at[0])
        wait_like(nrm.at[opposite, low], ag_f.at[1])
        wait_like(nrm.at[pl.ds(0, 3)], ag_snd.at[0])

        @pl.loop(0, n_shard)
        def _(d):
            value = jnp.dot(
                nrm[lax.rem(z + d, n_shard)], wup[...].reshape(n_path * rows, cols), preferred_element_type=F32
            )
            hid[d] = (value / (1.0 + jnp.exp(-value))).astype(BF16)

    def features(c):
        return pl.ds(pl.multiple_of(c * block, block), block)

    def rs_first(c):
        at = features(c)
        value = lax.dot_general(
            hid[...].reshape(n_shard * tokens, cols),
            wdn[c].reshape(block, cols),
            (((1,), (1,)), ((), ())),
            preferred_element_type=F32,
        ).astype(BF16)
        nrm[:, :, at] = value.reshape(n_shard, tokens, block)
        z_copy(nrm.at[2, top, at], rs_far.at[c, 0], rs_snd.at[0], s_rfar.at[c, 0], right)
        z_copy(nrm.at[2, low, at], rs_far.at[c, 1], rs_snd.at[0], s_rfar.at[c, 1], left)
        z_copy(nrm.at[1, low, at], rs_frm.at[c, 0, low], rs_snd.at[0], s_rfrm.at[c, 0], right)
        z_copy(nrm.at[3, top, at], rs_frm.at[c, 1, top], rs_snd.at[0], s_rfrm.at[c, 1], left)

    def rs_second(c):
        at = features(c)
        wait_like(rs_far.at[c, 0], s_rfar.at[c, 0])
        nrm[1, 0:half, at] = (nrm[1, 0:half, at].astype(F32) + rs_far[c, 0].astype(F32)).astype(BF16)
        z_copy(nrm.at[1, top, at], rs_frm.at[c, 0, top], rs_snd.at[0], s_rfrm.at[c, 0], right)
        wait_like(rs_far.at[c, 1], s_rfar.at[c, 1])
        nrm[3, half:tokens, at] = (nrm[3, half:tokens, at].astype(F32) + rs_far[c, 1].astype(F32)).astype(BF16)
        z_copy(nrm.at[3, low, at], rs_frm.at[c, 1, low], rs_snd.at[0], s_rfrm.at[c, 1], left)

    def rs_last(c):
        wait_like(rs_frm.at[c, 0], s_rfrm.at[c, 0])
        wait_like(rs_frm.at[c, 1], s_rfrm.at[c, 1])
        fit = lax.broadcasted_iota(jnp.int32, (TILE, 128), 1) // TILE == c
        per = 128 // TILE

        @pl.loop(0, tokens // TILE)
        def _(i):
            at = pl.ds(pl.multiple_of(i * TILE, TILE), TILE)
            for g in range(block // 128):
                lanes = pl.ds(g * 128, 128)
                total = (
                    nrm[0, at, pl.ds(pl.multiple_of(c * block + g * 128, 128), 128)].astype(F32)
                    + rs_frm[c, 0, at, lanes].astype(F32)
                    + rs_frm[c, 1, at, lanes].astype(F32)
                )
                for q in range(per):
                    place = pl.ds((g * per + q) * 128, 128)
                    moved = pltpu.roll(total, lax.rem(c + per - q, per) * TILE, 1)
                    old = out[at, place].astype(F32)
                    out[at, place] = jnp.where(fit, old + moved, old).astype(BF16)

    for j in range(AHEAD):
        send_deltas(j)

    @pl.loop(0, levels)
    def _(level):
        for m in range(choices):
            def count(p, total):
                named = jnp.where(table[level, p] == m, 1.0, 0.0)
                wts[(level * n_path + p) * choices + m] = named
                return total + named

            counts[level * choices + m] = lax.fori_loop(0, n_path, count, jnp.float32(0.0))

    load_x.wait()

    @pl.loop(0, tokens // TILE)
    def _(i):
        at = pl.ds(pl.multiple_of(i * TILE, TILE), TILE)
        xf = out[at, :].astype(F32)
        scale = lax.rsqrt(jnp.mean(xf * xf, axis=1, keepdims=True) + 1e-06)
        nrm[z, at, :] = (xf * scale).astype(BF16)

    z_copy(nrm.at[z, top], nrm.at[z, top], ag_snd.at[0], ag_l.at[0], right)
    z_copy(nrm.at[z, low], nrm.at[z, low], ag_snd.at[0], ag_r.at[1], left)
    z_copy(nrm.at[z, low], nrm.at[z, low], ag_snd.at[0], ag_l.at[1], right)
    z_copy(nrm.at[z, top], nrm.at[z, top], ag_snd.at[0], ag_r.at[0], left)
    load_m.wait()

    @pl.loop(0, jobs + 3)
    def _(n):
        def when(low_job, job, high_job, *steps):
            @pl.when((job >= low_job) & (job < high_job))
            def _():
                for step in steps:
                    step()

        when(0, n, jobs, lambda: step1(n))
        when(0, n + AHEAD, jobs, lambda: send_deltas(n + AHEAD))
        when(0, n - 1, jobs, lambda: step3(n - 1))
        when(0, n - 2, jobs, lambda: step5(n - 2))
        when(per_level, n - 3, jobs, lambda: rs_second(n - 3 - per_level))
        when(0, n, jobs, lambda: step2(n))
        when(0, n - 1, jobs, lambda: step4(n - 1))

        @pl.when(n == 4)
        def _():
            wait_like(nrm.at[left, top], ag_l.at[0])
            z_copy(nrm.at[left, top], nrm.at[left, top], ag_snd.at[0], ag_f.at[0], right)
            wait_like(nrm.at[right, low], ag_r.at[1])
            z_copy(nrm.at[right, low], nrm.at[right, low], ag_snd.at[0], ag_f.at[1], left)

        def arrived():
            for t in range(2):
                wait_like(rec.at[n - 2, t], s_b.at[n - 2, t])

        when(0, n - 2, jobs, arrived)
        when(per_level - 1, n - 2, per_level, first_projection)
        when(per_level, n - 2, jobs, lambda: rs_first(n - 2 - per_level))
        when(per_level, n - 3, jobs, lambda: rs_last(n - 3 - per_level))

    others = pl.ds(0, group - 1)
    wait_like(rec.at[:, :, others], o_a.at[0])
    wait_like(rec.at[:, :, others], o_b.at[0])
    wait_like(dense.at[:, :, pl.ds(0, 3)], o_bi.at[0])
    for j in range(jobs - SLOTS, jobs):
        wait_like(part.at[j % SLOTS], o_p.at[j])
    wait_like(nrm.at[pl.ds(0, 3)], rs_snd.at[0])


def per_device(path_table, master, momentum, deltas, activations):
    n_path = lax.axis_size("path")
    n_shard = lax.axis_size("shard")
    levels = deltas.shape[1]
    modules, rows, cols = master.shape
    choices = modules // levels
    tokens, width = activations.shape
    group = n_path // SIDE
    per_level = rows // TILE
    jobs = levels * per_level
    hbm = pl.BlockSpec(memory_space=pl.ANY)
    vmem = pl.BlockSpec(memory_space=pltpu.VMEM)
    smem = pl.BlockSpec(memory_space=pltpu.SMEM)
    dma = pltpu.SemaphoreType.DMA
    block = n_path * TILE
    wide = cols // 2
    return tuple(pl.pallas_call(
        kernel,
        out_shape=(
            jax.ShapeDtypeStruct((modules, rows, cols), F32),
            jax.ShapeDtypeStruct((tokens, width), BF16),
        ),
        in_specs=[smem, hbm, hbm, hbm, hbm],
        out_specs=(vmem, vmem),
        scratch_shapes=[
            pltpu.SMEM((levels * n_path * choices,), F32),
            pltpu.SMEM((modules,), F32),
            pltpu.VMEM((n_shard, tokens, width), BF16),
            pltpu.VMEM((SLOTS, choices, TILE, cols), F32),
            pltpu.VMEM((jobs, 2, group, SIDE, TILE, wide), BF16),
            pltpu.VMEM((SLOTS, 2, 3, choices, TILE, wide), BF16),
            pltpu.VMEM((jobs, 2, 2, choices // 2, TILE, wide), BF16),
            pltpu.VMEM((jobs, 2, 2, choices, TILE, wide), BF16),
            pltpu.VMEM((jobs, 2, SIDE, choices, TILE, wide), BF16),
            pltpu.VMEM((2, SIDE, choices, TILE, wide), BF16),
            pltpu.VMEM((SIDE, SIDE, 2, rows, cols), BF16),
            pltpu.VMEM((per_level, SIDE, SIDE, 2, TILE, cols), BF16),
            pltpu.VMEM((n_shard, tokens, cols), BF16),
            pltpu.VMEM((per_level, 2, tokens // 2, block), BF16),
            pltpu.VMEM((per_level, 2, tokens, block), BF16),
            dma((jobs, 2)), dma((jobs, 2, 2)), dma((jobs, 2, 2)), dma((jobs, 2)), dma((jobs, 2, 2)), dma((jobs, 2)),
            dma((1,)), dma((jobs,)), dma((1,)), dma((1,)),
            dma((1,)), dma((2,)), dma((2,)), dma((2,)),
            dma((1,)), dma((per_level, 2)), dma((per_level, 2)),
            dma((2,)), dma((SLOTS,)),
        ],
        compiler_params=pltpu.CompilerParams(
            collective_id=0, has_side_effects=True, vmem_limit_bytes=62 * 1024 * 1024
        ),
    )(
        path_table.T,
        master,
        momentum,
        deltas.reshape(levels, SIDE, SIDE, 2, rows, cols),
        activations,
    ))


def solution(mesh):
    placed = (
        P(),
        P(None, "path", "shard"),
        P(None, "path", "shard"),
        P("path", None, None, "shard"),
        P(("path", "shard"), None),
    )
    return jax.shard_map(
        per_device,
        mesh=mesh,
        in_specs=placed,
        out_specs=(P(None, "path", "shard"), P(("path", "shard"), None)),
        check_vma=False,
    )
```

time: 398 us -> 248 us (0.62)
  Pallas kernels: 0 us -> 241 us
  waiting for transfers between devices: 172 us -> 0 us
  blocking collectives: 107 us -> 0 us
  local copies, waits for them, and re-layouts: 51.1 us -> 6.28 us
  matrix products: 38.2 us -> 0 us
  between operations: 14.1 us -> 0.65 us
  starting transfers between devices: 8.87 us -> 0 us
  other arithmetic: 6.63 us -> 0 us
    pallas_call x0 -> x1, Pallas kernels: none -> 241 us  [per_device(): pl.pallas_call(kernel, out_shape=(jax.ShapeDtypeStruct((modules, rows, co...]
    all_to_all x1 -> x0, blocking collectives: 107 us -> none  [per_device(): lax.all_to_all(outgoing, 'path', split_axis=0, concat_axis=2, tiled=True)]
    all_to_all x1 -> x0, waiting for transfers between devices: 96.8 us -> none  [per_device(): lax.all_to_all(deltas, 'path', split_axis=2, concat_axis=0, tiled=True)]
    reduce_scatter x1 -> x0, waiting for transfers between devices: 74.8 us -> none  [per_device(): lax.psum_scatter(lax.dot_general(hidden, w_down, (((1,), (1,)), ((), ()))...]
    dot_general x3 -> x0, matrix products: 38.2 us -> none  [the longest x1 16.7 us: per_device(): jnp.dot(picks_half, received.reshape(path_count * levels, state_rows * co...]
    unnamed x9 -> x4, local copies, waits for them, and re-layouts: 34.5 us -> 6.28 us
    all_to_all x2 -> x0, local copies, waits for them, and re-layouts: 16.3 us -> none  [the longest x1 8.69 us: per_device(): lax.all_to_all(deltas, 'path', split_axis=2, concat_axis=0, tiled=True)]
    all_to_all x1 -> x0, starting transfers between devices: 8.78 us -> none  [per_device(): lax.all_to_all(deltas, 'path', split_axis=2, concat_axis=0, tiled=True)]
  transfers between devices with their start and end apart: 3 -> 0, of which waited for: 2 -> 0; matrix products, arithmetic and copies ran while one was open for 15% -> 0% of each run, Pallas kernels for 0% -> 0%
where the time goes in v2:
time: 248 us
  Pallas kernels  241 us (97%)
  local copies, waits for them, and re-layouts  6.28 us (3%)
    pallas_call x1, Pallas kernels, per_device(): pl.pallas_call(kernel, out_shape=(jax.ShapeDtypeStruct((modules, rows, co...  241 us
    unnamed x4, local copies, waits for them, and re-layouts  6.28 us

profile of v2, /device:TPU:1, one launch (start us, length us, event | category | flops | bytes accessed | tf_op | source)
XLA Modules:
  0.0 248.3 jit_solution(82106648927555416)
XLA Ops:
  0.6 241.4 %shard_map.68 = (f32[16,128,512]{2,1,0:T(8,128)}, bf16[256,4096]{1,0:T(8,128)(2,1)}) custom-call(s32[2,32]{1,0:T(2,128)} %bitcast.3, f32[16,128,512]{2,1,0:T(8,128)} %master.1, f32[16,128,512]{2,1,0:T(8,128)} %momentum.1, bf16[2,4,4,2,128,512]{5,4,3,2,1,0:T(8,128)(2,1)} %bitcast.2, bf16[256,4096]{1,0:T(8,128)(2,1)} %acts.1), custom_call_target="tpu_custom_call" | custom-call | tf_op jit(solution)/shard_map/pallas_call | solution.py:411
  242.0 0.0 copy-start
  242.0 5.0 %copy.9 = f32[16,128,512]{2,1,0:T(8,128)} copy(f32[16,128,512]{2,1,0:T(8,128)} %get-tuple-element.4) | data formatting | bytes 8388608
  247.0 0.0 copy-done
  247.0 1.3 copy.10
Async XLA Ops:
  242.0 5.0 %copy-start = (bf16[256,4096]{1,0:T(8,128)(2,1)S(1)}, bf16[256,4096]{1,0:T(8,128)(2,1)}, u32[]{:S(2)}) copy-start(bf16[256,4096]{1,0:T(8,128)(2,1)} %get-tuple-element.5) | copy-start | bytes 6291460

commit v3 on v2

--- a/solution.py
+++ b/solution.py
@@ -11,7 +11,7 @@
 
 TILE = 16
 SLOTS = 4
-AHEAD = 3
+AHEAD = 2
 SIDE = 4
 
 
@@ -351,7 +351,7 @@
     z_copy(nrm.at[z, top], nrm.at[z, top], ag_snd.at[0], ag_r.at[0], left)
     load_m.wait()
 
-    @pl.loop(0, jobs + 3)
+    @pl.loop(0, jobs + 4)
     def _(n):
         def when(low_job, job, high_job, *steps):
             @pl.when((job >= low_job) & (job < high_job))
@@ -359,14 +359,21 @@
                 for step in steps:
                     step()
 
-        when(0, n, jobs, lambda: step1(n))
-        when(0, n + AHEAD, jobs, lambda: send_deltas(n + AHEAD))
+        when(0, n - 0, jobs, lambda: step1(n - 0))
         when(0, n - 1, jobs, lambda: step3(n - 1))
         when(0, n - 2, jobs, lambda: step5(n - 2))
-        when(per_level, n - 3, jobs, lambda: rs_second(n - 3 - per_level))
-        when(0, n, jobs, lambda: step2(n))
+        when(0, n + AHEAD, jobs, lambda: send_deltas(n + AHEAD))
+
+        def arrived():
+            for t in range(2):
+                wait_like(rec.at[n - 3, t], s_b.at[n - 3, t])
+
+        when(0, n - 3, jobs, arrived)
+        when(per_level - 1, n - 3, per_level, first_projection)
+        when(per_level, n - 3, jobs, lambda: rs_first(n - 3 - per_level))
+        when(per_level, n - 4, jobs, lambda: rs_last(n - 4 - per_level))
+        when(0, n - 0, jobs, lambda: step2(n - 0))
         when(0, n - 1, jobs, lambda: step4(n - 1))
-
         @pl.when(n == 4)
         def _():
             wait_like(nrm.at[left, top], ag_l.at[0])
@@ -374,14 +381,7 @@
             wait_like(nrm.at[right, low], ag_r.at[1])
             z_copy(nrm.at[right, low], nrm.at[right, low], ag_snd.at[0], ag_f.at[1], left)
 
-        def arrived():
-            for t in range(2):
-                wait_like(rec.at[n - 2, t], s_b.at[n - 2, t])
-
-        when(0, n - 2, jobs, arrived)
-        when(per_level - 1, n - 2, per_level, first_projection)
-        when(per_level, n - 2, jobs, lambda: rs_first(n - 2 - per_level))
-        when(per_level, n - 3, jobs, lambda: rs_last(n - 3 - per_level))
+        when(per_level, n - 3, jobs, lambda: rs_second(n - 3 - per_level))
 
     others = pl.ds(0, group - 1)
     wait_like(rec.at[:, :, others], o_a.at[0])
@@ -411,8 +411,8 @@
     return tuple(pl.pallas_call(
         kernel,
         out_shape=(
-            jax.ShapeDtypeStruct((modules, rows, cols), F32),
-            jax.ShapeDtypeStruct((tokens, width), BF16),
+            pltpu.VMEM((modules, rows, cols), F32),
+            pltpu.VMEM((tokens, width), BF16),
         ),
         in_specs=[smem, hbm, hbm, hbm, hbm],
         out_specs=(vmem, vmem),
@@ -439,7 +439,7 @@
             dma((2,)), dma((SLOTS,)),
         ],
         compiler_params=pltpu.CompilerParams(
-            collective_id=0, has_side_effects=True, vmem_limit_bytes=62 * 1024 * 1024
+            collective_id=0, has_side_effects=True, vmem_limit_bytes=56 * 1024 * 1024
         ),
     )(
         path_table.T,

time: 248 us -> 209 us (0.84); the launches traced: 248 us -> 207 us
  Pallas kernels: 241 us -> 203 us
  local copies, waits for them, and re-layouts: 6.28 us -> 3.33 us
    pallas_call x1, Pallas kernels: 241 us -> 203 us  [per_device(): pl.pallas_call(kernel, out_shape=(pltpu.VMEM((modules, rows, cols), F32),...]
    unnamed x4 -> x2, local copies, waits for them, and re-layouts: 6.28 us -> 3.33 us
where the time goes in v3:
time: 209 us; the launch traced here: 207 us
  Pallas kernels  203 us (97%)
  local copies, waits for them, and re-layouts  3.33 us (2%)
    pallas_call x1, Pallas kernels, per_device(): pl.pallas_call(kernel, out_shape=(pltpu.VMEM((modules, rows, cols), F32),...  203 us

profile of v3, /device:TPU:1, one launch (start us, length us, event | category | flops | bytes accessed | tf_op | source)
XLA Modules:
  0.0 206.7 jit_solution(8090481259046702840)
XLA Ops:
  0.6 202.7 %shard_map.68 = (f32[16,128,512]{2,1,0:T(8,128)S(1)}, bf16[256,4096]{1,0:T(8,128)(2,1)S(1)}) custom-call(s32[2,32]{1,0:T(2,128)} %bitcast.3, f32[16,128,512]{2,1,0:T(8,128)} %master.1, f32[16,128,512]{2,1,0:T(8,128)} %momentum.1, bf16[2,4,4,2,128,512]{5,4,3,2,1,0:T(8,128)(2,1)} %bitcast.2, bf16[256,4096]{1,0:T(8,128)(2,1)} %acts.1), custom_call_target="tpu_custom_call" | custom-call | tf_op jit(solution)/shard_map/pallas_call | solution.py:411
  203.3 2.0 copy.9
  205.3 1.3 copy.10

commit v4 on v3

--- a/solution.py
+++ b/solution.py
@@ -271,7 +271,7 @@
         @pl.loop(0, n_shard)
         def _(d):
             value = jnp.dot(
-                nrm[lax.rem(z + d, n_shard)], wup[...].reshape(n_path * rows, cols), preferred_element_type=F32
+                nrm[lax.rem(z + 2 + 3 * d, n_shard)], wup[...].reshape(n_path * rows, cols), preferred_element_type=F32
             )
             hid[d] = (value / (1.0 + jnp.exp(-value))).astype(BF16)
 
@@ -280,15 +280,20 @@
 
     def rs_first(c):
         at = features(c)
-        value = lax.dot_general(
-            hid[...].reshape(n_shard * tokens, cols),
-            wdn[c].reshape(block, cols),
-            (((1,), (1,)), ((), ())),
-            preferred_element_type=F32,
-        ).astype(BF16)
-        nrm[:, :, at] = value.reshape(n_shard, tokens, block)
-        z_copy(nrm.at[2, top, at], rs_far.at[c, 0], rs_snd.at[0], s_rfar.at[c, 0], right)
-        z_copy(nrm.at[2, low, at], rs_far.at[c, 1], rs_snd.at[0], s_rfar.at[c, 1], left)
+
+        def product(first_block, count):
+            value = lax.dot_general(
+                hid[first_block:first_block + count].reshape(count * tokens, cols),
+                wdn[c].reshape(block, cols),
+                (((1,), (1,)), ((), ())),
+                preferred_element_type=F32,
+            ).astype(BF16)
+            nrm[first_block:first_block + count, :, at] = value.reshape(count, tokens, block)
+
+        product(0, 1)
+        z_copy(nrm.at[0, top, at], rs_far.at[c, 0], rs_snd.at[0], s_rfar.at[c, 0], right)
+        z_copy(nrm.at[0, low, at], rs_far.at[c, 1], rs_snd.at[0], s_rfar.at[c, 1], left)
+        product(1, 3)
         z_copy(nrm.at[1, low, at], rs_frm.at[c, 0, low], rs_snd.at[0], s_rfrm.at[c, 0], right)
         z_copy(nrm.at[3, top, at], rs_frm.at[c, 1, top], rs_snd.at[0], s_rfrm.at[c, 1], left)
 
@@ -313,15 +318,15 @@
             for g in range(block // 128):
                 lanes = pl.ds(g * 128, 128)
                 total = (
-                    nrm[0, at, pl.ds(pl.multiple_of(c * block + g * 128, 128), 128)].astype(F32)
+                    nrm[2, at, pl.ds(pl.multiple_of(c * block + g * 128, 128), 128)].astype(F32)
                     + rs_frm[c, 0, at, lanes].astype(F32)
                     + rs_frm[c, 1, at, lanes].astype(F32)
                 )
+                places = [pl.ds((g * per + q) * 128, 128) for q in range(per)]
+                olds = [out[at, place].astype(F32) for place in places]
+                moved = [pltpu.roll(total, lax.rem(c + per - q, per) * TILE, 1) for q in range(per)]
                 for q in range(per):
-                    place = pl.ds((g * per + q) * 128, 128)
-                    moved = pltpu.roll(total, lax.rem(c + per - q, per) * TILE, 1)
-                    old = out[at, place].astype(F32)
-                    out[at, place] = jnp.where(fit, old + moved, old).astype(BF16)
+                    out[at, places[q]] = jnp.where(fit, olds[q] + moved[q], olds[q]).astype(BF16)
 
     for j in range(AHEAD):
         send_deltas(j)
@@ -351,7 +356,7 @@
     z_copy(nrm.at[z, top], nrm.at[z, top], ag_snd.at[0], ag_r.at[0], left)
     load_m.wait()
 
-    @pl.loop(0, jobs + 4)
+    @pl.loop(0, jobs + 5)
     def _(n):
         def when(low_job, job, high_job, *steps):
             @pl.when((job >= low_job) & (job < high_job))
@@ -359,21 +364,17 @@
                 for step in steps:
                     step()
 
-        when(0, n - 0, jobs, lambda: step1(n - 0))
-        when(0, n - 1, jobs, lambda: step3(n - 1))
-        when(0, n - 2, jobs, lambda: step5(n - 2))
-        when(0, n + AHEAD, jobs, lambda: send_deltas(n + AHEAD))
+        when(0, n - 2, jobs, lambda: step3(n - 2))
 
         def arrived():
             for t in range(2):
-                wait_like(rec.at[n - 3, t], s_b.at[n - 3, t])
-
-        when(0, n - 3, jobs, arrived)
-        when(per_level - 1, n - 3, per_level, first_projection)
-        when(per_level, n - 3, jobs, lambda: rs_first(n - 3 - per_level))
-        when(per_level, n - 4, jobs, lambda: rs_last(n - 4 - per_level))
-        when(0, n - 0, jobs, lambda: step2(n - 0))
-        when(0, n - 1, jobs, lambda: step4(n - 1))
+                wait_like(rec.at[n - 4, t], s_b.at[n - 4, t])
+
+        when(0, n - 4, jobs, arrived)
+        when(per_level, n - 4, jobs, lambda: rs_first(n - 4 - per_level))
+        when(0, n - 1, jobs, lambda: step2(n - 1))
+        when(0, n - 3, jobs, lambda: step5(n - 3))
+        when(0, n, jobs, lambda: step1(n))
         @pl.when(n == 4)
         def _():
             wait_like(nrm.at[left, top], ag_l.at[0])
@@ -381,7 +382,11 @@
             wait_like(nrm.at[right, low], ag_r.at[1])
             z_copy(nrm.at[right, low], nrm.at[right, low], ag_snd.at[0], ag_f.at[1], left)
 
-        when(per_level, n - 3, jobs, lambda: rs_second(n - 3 - per_level))
+        when(per_level, n - 5, jobs, lambda: rs_last(n - 5 - per_level))
+        when(per_level, n - 4, jobs, lambda: rs_second(n - 4 - per_level))
+        when(per_level - 1, n - 4, per_level, first_projection)
+        when(0, n - 2, jobs, lambda: step4(n - 2))
+        when(0, n + AHEAD, jobs, lambda: send_deltas(n + AHEAD))
 
     others = pl.ds(0, group - 1)
     wait_like(rec.at[:, :, others], o_a.at[0])

time: 209 us -> 203 us (0.971); the launches traced: 207 us -> 203 us
  Pallas kernels: 203 us -> 199 us
    pallas_call x1, Pallas kernels: 203 us -> 199 us  [per_device(): pl.pallas_call(kernel, out_shape=(pltpu.VMEM((modules, rows, cols), F32),...]
where the time goes in v4:
time: 203 us
  Pallas kernels  199 us (98%)
  local copies, waits for them, and re-layouts  3.33 us (2%)
    pallas_call x1, Pallas kernels, per_device(): pl.pallas_call(kernel, out_shape=(pltpu.VMEM((modules, rows, cols), F32),...  199 us

profile of v4, /device:TPU:1, one launch (start us, length us, event | category | flops | bytes accessed | tf_op | source)
XLA Modules:
  0.0 203.0 jit_solution(17658578337135647014)
XLA Ops:
  0.6 199.1 %shard_map.68 = (f32[16,128,512]{2,1,0:T(8,128)S(1)}, bf16[256,4096]{1,0:T(8,128)(2,1)S(1)}) custom-call(s32[2,32]{1,0:T(2,128)} %bitcast.3, f32[16,128,512]{2,1,0:T(8,128)} %master.1, f32[16,128,512]{2,1,0:T(8,128)} %momentum.1, bf16[2,4,4,2,128,512]{5,4,3,2,1,0:T(8,128)(2,1)} %bitcast.2, bf16[256,4096]{1,0:T(8,128)(2,1)} %acts.1), custom_call_target="tpu_custom_call" | custom-call | tf_op jit(solution)/shard_map/pallas_call | solution.py:416
  199.7 2.0 copy.9
  201.7 1.3 copy.10

commit v5 on v4

--- a/solution.py
+++ b/solution.py
@@ -328,7 +328,7 @@
                 for q in range(per):
                     out[at, places[q]] = jnp.where(fit, olds[q] + moved[q], olds[q]).astype(BF16)
 
-    for j in range(AHEAD):
+    for j in range(AHEAD + 1):
         send_deltas(j)
 
     @pl.loop(0, levels)
@@ -382,11 +382,11 @@
             wait_like(nrm.at[right, low], ag_r.at[1])
             z_copy(nrm.at[right, low], nrm.at[right, low], ag_snd.at[0], ag_f.at[1], left)
 
-        when(per_level, n - 5, jobs, lambda: rs_last(n - 5 - per_level))
-        when(per_level, n - 4, jobs, lambda: rs_second(n - 4 - per_level))
         when(per_level - 1, n - 4, per_level, first_projection)
         when(0, n - 2, jobs, lambda: step4(n - 2))
-        when(0, n + AHEAD, jobs, lambda: send_deltas(n + AHEAD))
+        when(AHEAD + 1, n + AHEAD, jobs, lambda: send_deltas(n + AHEAD))
+        when(per_level, n - 4, jobs, lambda: rs_second(n - 4 - per_level))
+        when(per_level, n - 5, jobs, lambda: rs_last(n - 5 - per_level))
 
     others = pl.ds(0, group - 1)
     wait_like(rec.at[:, :, others], o_a.at[0])

time: 203 us -> 202 us (level)
  no operation moved by 1% of the time
where the time goes in v5:
time: 202 us; the launch traced here: 201 us
  Pallas kernels  197 us (98%)
  local copies, waits for them, and re-layouts  3.33 us (2%)
    pallas_call x1, Pallas kernels, per_device(): pl.pallas_call(kernel, out_shape=(pltpu.VMEM((modules, rows, cols), F32),...  197 us

profile of v5, /device:TPU:1, one launch (start us, length us, event | category | flops | bytes accessed | tf_op | source)
XLA Modules:
  0.0 201.1 jit_solution(17312811443551228304)
XLA Ops:
  0.6 197.1 %shard_map.68 = (f32[16,128,512]{2,1,0:T(8,128)S(1)}, bf16[256,4096]{1,0:T(8,128)(2,1)S(1)}) custom-call(s32[2,32]{1,0:T(2,128)} %bitcast.3, f32[16,128,512]{2,1,0:T(8,128)} %master.1, f32[16,128,512]{2,1,0:T(8,128)} %momentum.1, bf16[2,4,4,2,128,512]{5,4,3,2,1,0:T(8,128)(2,1)} %bitcast.2, bf16[256,4096]{1,0:T(8,128)(2,1)} %acts.1), custom_call_target="tpu_custom_call" | custom-call | tf_op jit(solution)/shard_map/pallas_call | solution.py:416
  197.7 2.0 %copy.9 = f32[16,128,512]{2,1,0:T(8,128)} copy(f32[16,128,512]{2,1,0:T(8,128)S(1)} %get-tuple-element.2) | data formatting | bytes 8388608
  199.8 1.3 copy.10
